TPU v7x, 512 devices: a whole 4x4x16 slice. The times are simulated.
512 devices in a mesh: row: 16 (over y, x), col: 32 (over z, core).
Axes of the slice: x: 4, y: 4, z: 16, core: 2. Of those that a mesh axis runs over, the one named last changes fastest.
Arguments:
- momentum: float32 [4608, 8192], P('row', 'col'), may hold values from -37 to 37
Outputs:
- update: float32 [4608, 8192], P('row', 'col')
All inputs are finite; a program needn't handle non-finite values.
Results may differ from a plain program's by a relative error of at most 0.0049.
Values may be sent and summed in bfloat16 or wider, within the bound.
A program may use at most 64 MiB of HBM per device.

v0:
```python
import math

import jax
import jax.numpy as jnp
from jax import lax
from jax.sharding import PartitionSpec as P

ROWS = 4608
COLS = 8192


quintic_a = 3.4445
quintic_b = -4.775
quintic_c = 2.0315


def from_root(shard, axis, root):
    mine = lax.axis_index(axis) == root
    return lax.psum(jnp.where(mine, shard, jnp.zeros_like(shard)), axis)


def rows_product(left, right):
    return lax.dot_general(
        left, right, (((1,), (1,)), ((), ())), preferred_element_type=jnp.float32
    )


def body(momentum):
    partial_sum = jnp.sum(momentum * momentum)
    norm_squares = lax.psum(partial_sum, ("row", "col"))
    factor = 0.6 * math.sqrt(ROWS) / (jnp.sqrt(norm_squares) + 1e-07)
    scaled = (momentum * factor).astype(jnp.bfloat16)
    tile_ratio = lax.axis_size("col") // lax.axis_size("row")
    col_index = lax.axis_index("col")
    source_row = col_index // tile_ratio
    half_index = col_index % tile_ratio
    row_panel = lax.all_gather(scaled, "col", axis=1, tiled=True)
    part_rows = row_panel.shape[0] // tile_ratio
    own_part = lax.dynamic_slice_in_dim(row_panel, half_index * part_rows, part_rows, 0)
    peer_rows = from_root(own_part, "row", source_row)
    gram = rows_product(row_panel, peer_rows).astype(jnp.bfloat16)
    gram_panel = lax.all_gather(gram, "col", axis=1, tiled=True)
    gram_columns = lax.all_gather(gram, "row", axis=0, tiled=True)
    squared = jnp.dot(gram_panel, gram_columns, preferred_element_type=jnp.float32)
    poly = (quintic_b * gram.astype(jnp.float32) + quintic_c * squared).astype(jnp.bfloat16)
    poly_panel = lax.all_gather(poly, "col", axis=1, tiled=True)
    product = jnp.dot(
        poly_panel,
        lax.all_gather(scaled, "row", axis=0, tiled=True),
        preferred_element_type=jnp.float32,
    )
    return math.sqrt(COLS) * (quintic_a * scaled.astype(jnp.float32) + product)


def solution(mesh):
    placed = (P("row", "col"),)
    return jax.shard_map(
        body, mesh=mesh, in_specs=placed, out_specs=P("row", "col"), check_vma=False
    )
```

profile of v0, /device:TPU:1, one launch (start us, length us, event | category | flops | bytes accessed | tf_op | source)
XLA Modules:
  0.0 607.3 jit_solution(2333956670961168290)
XLA Ops:
  6.5 0.0 all-gather.7.cloned.1.call-start
  6.5 1.6 multiply_reduce_fusion
  8.2 111.0 %psum.14 = f32[]{:T(128)} all-reduce(f32[]{:T(128)} %multiply_reduce_fusion), channel_id=1, replica_groups=mesh['row'=16,'col'=32] {'row','col'}, use_global_device_ids=true, to_apply=%region_1.0 | all-reduce | flops 1 | bytes 8 | tf_op jit(solution)/shard_map/psum | solution.py:30
  119.9 1.6 multiply_convert_fusion
  121.5 0.0 all-gather.7.cloned.1.call-update
  121.6 0.0 all-reduce.2.cloned.1.call-start
  121.6 75.4 %all-gather.7.cloned.1.call-done = bf16[288,8192]{1,0:T(8,128)(2,1)} async-done(((bf16[288,256]{1,0:T(8,128)(2,1)}), bf16[288,8192]{1,0:T(8,128)(2,1)}) %all-gather.7.cloned.1.call-update) | async-done | bytes 4718608 | tf_op jit(solution)/shard_map/all_gather | solution.py:37
  197.0 3.6 dynamic-slice_select_fusion
  200.6 0.0 all-reduce.2.cloned.1.call-update
  200.6 0.0 all-gather.15.cloned.1.call-start
  200.7 117.7 %all-reduce.2.cloned.1.call-done = bf16[144,8192]{1,0:T(8,128)(2,1)} async-done(((bf16[144,8192]{1,0:T(8,128)(2,1)}), bf16[144,8192]{1,0:T(8,128)(2,1)}) %all-reduce.2.cloned.1.call-update) | async-done | bytes 2359312 | tf_op jit(solution)/shard_map/psum | solution.py:19
  318.4 5.8 convolution_convert_fusion
  324.1 0.0 all-gather.15.cloned.1.call-update
  324.1 0.0 all-gather.9.cloned.1.call-start
  324.2 0.5 all-gather.9.cloned.1.call-update
  324.7 0.0 all-gather.13.cloned.1.call-start
  324.8 0.5 all-gather.13.cloned.1.call-update
  325.3 0.0 all-gather.11.cloned.1.call-start
  325.4 57.5 %all-gather.15.cloned.1.call-done = bf16[16,288,144]{1,2,0:T(8,128)(2,1)} async-done(((bf16[1,288,144]{1,2,0:T(8,128)(2,1)}), bf16[16,288,144]{1,2,0:T(8,128)(2,1)}) %all-gather.15.cloned.1.call-update) | async-done | bytes 1327120 | tf_op jit(solution)/shard_map/all_gather | solution.py:43
  382.9 1.9 copy.3
  384.8 0.0 copy-start.1
  384.8 1.9 reshape.1
  386.7 0.0 copy-start
  386.7 73.0 %all-gather.9.cloned.1.call-done = bf16[288,4608]{0,1:T(8,128)(2,1)} async-done(((bf16[288,144]{0,1:T(8,128)(2,1)}), bf16[288,4608]{0,1:T(8,128)(2,1)}) %all-gather.9.cloned.1.call-update) | async-done | bytes 2654224 | tf_op jit(solution)/shard_map/all_gather | solution.py:42
  459.7 0.0 copy-done.1
  459.7 3.5 fusion.2
  463.2 0.0 all-gather.11.cloned.1.call-update
  463.2 56.3 %all-gather.13.cloned.1.call-done = bf16[4608,256]{1,0:T(8,128)(2,1)} async-done(((bf16[288,256]{1,0:T(8,128)(2,1)}), bf16[4608,256]{1,0:T(8,128)(2,1)}) %all-gather.13.cloned.1.call-update) | async-done | bytes 2359312 | tf_op jit(solution)/shard_map/all_gather | solution.py:49
  519.5 76.3 %all-gather.11.cloned.1.call-done = bf16[288,4608]{0,1:T(8,128)(2,1)} async-done(((bf16[288,144]{0,1:T(8,128)(2,1)}), bf16[288,4608]{0,1:T(8,128)(2,1)}) %all-gather.11.cloned.1.call-update) | async-done | bytes 2654224 | tf_op jit(solution)/shard_map/all_gather | solution.py:46
  595.8 0.0 copy-done
  595.8 4.6 fusion
Async XLA Ops:
  6.5 190.5 %all-gather.7.cloned.1.call-start = ((), (), s32[]{:S(2)}) async-start(), calls=%async_computation | async-start | bytes 4866048 | tf_op jit(solution)/shard_map/all_gather | solution.py:37
  121.6 196.8 %all-reduce.2.cloned.1.call-start = ((), (), s32[]{:S(2)}) async-start(), calls=%async_computation.1 | async-start | bytes 4718592 | tf_op jit(solution)/shard_map/psum | solution.py:19
  200.6 182.2 %all-gather.15.cloned.1.call-start = ((), (), s32[]{:S(2)}) async-start(), calls=%async_computation.5 | async-start | bytes 1880064 | tf_op jit(solution)/shard_map/all_gather | solution.py:43
  324.1 135.5 %all-gather.9.cloned.1.call-start = ((), (), s32[]{:S(2)}) async-start(), calls=%async_computation.2 | async-start | bytes 3649536 | tf_op jit(solution)/shard_map/all_gather | solution.py:42
  324.7 194.8 %all-gather.13.cloned.1.call-start = ((), (), s32[]{:S(2)}) async-start(), calls=%async_computation.4 | async-start | bytes 2506752 | tf_op jit(solution)/shard_map/all_gather | solution.py:49
  325.3 270.5 %all-gather.11.cloned.1.call-start = ((), (), s32[]{:S(2)}) async-start(), calls=%async_computation.3 | async-start | bytes 3649536 | tf_op jit(solution)/shard_map/all_gather | solution.py:46
  384.8 74.9 %copy-start.1 = (bf16[288,144]{0,1:T(8,128)(2,1)S(1)}, bf16[288,144]{0,1:T(8,128)(2,1)}, u32[]{:S(2)}) copy-start(bf16[288,144]{0,1:T(8,128)(2,1)} %convolution_convert_fusion) | copy-start | bytes 248836
  386.7 209.2 %copy-start = (bf16[288,256]{1,0:T(8,128)(2,1)S(1)}, bf16[288,256]{1,0:T(8,128)(2,1)}, u32[]{:S(2)}) copy-start(bf16[288,256]{1,0:T(8,128)(2,1)} %multiply_convert_fusion) | copy-start | bytes 442372
Sparse Core Ops, SparseCore 0:
  121.7 75.3 all-gather.6
  200.8 117.5 all-reduce.1
  324.3 58.5 all-gather.14
  385.1 74.5 all-gather.8
  463.0 56.4 all-gather.12
  521.7 74.0 all-gather.10
where the time goes:
time: 608 us; the launch traced here: 607 us
  waiting for transfers between devices  457 us (75%)
  blocking collectives  111 us (18%)
  between operations  14.3 us (2%)
  matrix products  13.9 us (2%)
  other arithmetic  6.87 us (1%)
    psum x1, waiting for transfers between devices, from_root(): return lax.psum(jnp.where(mine, shard, jnp.zeros_like(shard)), axis)  118 us
    psum x1, blocking collectives, body(): norm_squares = lax.psum(partial_sum, ('row', 'col'))  111 us
    all_gather x1, waiting for transfers between devices, body(): poly_panel = lax.all_gather(poly, 'col', axis=1, tiled=True)  76.3 us
    all_gather x1, waiting for transfers between devices, body(): row_panel = lax.all_gather(scaled, 'col', axis=1, tiled=True)  75.4 us
    all_gather x1, waiting for transfers between devices, body(): gram_panel = lax.all_gather(gram, 'col', axis=1, tiled=True)  73 us
    all_gather x1, waiting for transfers between devices, body(): gram_columns = lax.all_gather(gram, 'row', axis=0, tiled=True)  57.5 us
    all_gather x1, waiting for transfers between devices, body(): lax.all_gather(scaled, 'row', axis=0, tiled=True)  56.3 us
  transfers between devices with their start and end apart: 6, of which 6 were waited for; matrix products, arithmetic and copies ran while one was open for 1% of the time, Pallas kernels for 0%

commit v1 on v0

v1 whole, which is shorter than its diff:
```python
import functools
import math

import jax
import jax.numpy as jnp
from jax import lax
from jax.experimental import pallas as pl
from jax.experimental.pallas import tpu as pltpu
from jax.sharding import PartitionSpec as P

ROWS = 4608
COLS = 8192

quintic_a = 3.4445
quintic_b = -4.775
quintic_c = 2.0315

MESH = pl.DeviceIdType.MESH
F32 = jnp.float32
BF16 = jnp.bfloat16

BLOCK = 288
WIDTH = 256
PANEL = 4 * BLOCK
HALF = PANEL // 2
GROUP = 384
GROUPS = PANEL // GROUP
CHUNK = 112
STACK = 16 * CHUNK
PARTS = ((0, 64), (64, 48))
NP = len(PARTS)
STEP4 = (1, 3, 2)


def rows_product(left, right):
    return lax.dot_general(left, right, (((1,), (1,)), ((), ())), preferred_element_type=F32)


def columns_product(left, right):
    return lax.dot_general(left, right, (((0,), (0,)), ((), ())), preferred_element_type=F32)


def kernel(
    m_ref,
    out_ref,
    row_f, col_f, row_o, col_o,
    row_b, col_b, row_ob, col_ob,
    part, gram, ring_p, ring_m,
    tiles, tile_in,
    w, wb, wb2, y_all, y_in, z_in, y_own,
    tile_s, tile_r, bulk_s, bulk_r, pass_s, pass_r,
    rs_s, rs_r, ag_s, ag_r, swap_s, swap_r,
    ys_s, ys_r, yg_s, yg_r, zs_s, zs_r,
):
    row, col = lax.axis_index("row"), lax.axis_index("col")
    y, x, z, k = row // 4, row % 4, col // 2, col % 2

    def at_x(d):
        return (y * 4 + (x + d) % 4, col)

    def at_y(d):
        return (((y + d) % 4) * 4 + x, col)

    def at_z(d):
        return (row, ((z + d) % 16) * 2 + k)

    other = (row, z * 2 + 1 - k)

    def send(src, dst, ss, rs, device):
        return pltpu.make_async_remote_copy(
            src_ref=src, dst_ref=dst, send_sem=ss, recv_sem=rs, device_id=device, device_id_type=MESH
        )

    sent = []

    barrier = pltpu.get_barrier_semaphore()
    peers = [at_x(d) for d in STEP4] + [at_y(d) for d in STEP4] + [other]
    peers += [at_z(d) for d in (1, 15, 2, 14, 4, 12)]
    for peer in peers:
        pl.semaphore_signal(barrier, inc=1, device_id=peer, device_id_type=MESH)

    squares = m_ref[...] * m_ref[...]
    squares = jnp.sum(squares.reshape(BLOCK // 8, 8, WIDTH), axis=0)
    tiles[0] = squares[:, :128] + squares[:, 128:]
    part[STACK - 64 : STACK, :] = jnp.zeros((64, GROUP), F32)

    pl.semaphore_wait(barrier, len(peers))

    def tile_copy(stage, slot, device, src=None):
        src = tiles.at[stage] if src is None else src
        return send(src, tile_in.at[slot], tile_s.at[slot], tile_r.at[slot], device)

    def exchange(stage, slots):
        for slot, device in slots:
            c = tile_copy(stage, slot, device)
            c.start()
            sent.append(c)

    def block(ref, t, rows=BLOCK):
        return ref.at[pl.ds(pl.multiple_of(t * rows, 16), rows), :]

    z1 = [(0, at_z(1)), (1, at_z(15)), (2, at_z(2))]
    exchange(0, z1)
    bulk = []
    for i, d in enumerate(STEP4):
        for j, (dst, here, device) in enumerate(((row_f, x, at_x(d)), (col_f, y, at_y(d)))):
            c = send(m_ref, block(dst, here), bulk_s.at[j, i], bulk_r.at[j, i], device)
            c.start()
            sent.append(c)
            bulk.append(c)

    def pass_rows(src, t):
        c = send(src, block(row_o, t % 2), pass_s.at[0, t % 2], pass_r.at[0, t % 2], other)

        @pl.when(t // 2 != k)
        def _():
            c.start()

    def pass_cols(src, t):
        c = send(src, block(col_o, t), pass_s.at[1, t], pass_r.at[1, t], other)
        c.start()

    pass_rows(m_ref, x)
    pass_cols(m_ref, y)

    def gather_tiles(slots):
        for slot, device in slots:
            tile_copy(0, slot, device).wait_recv()

    gather_tiles(z1)
    tiles[1] = tiles[0] + tile_in[0] + tile_in[1] + tile_in[2]
    z2 = [(3, at_z(4)), (4, at_z(12))]
    exchange(1, z2)
    gather_tiles(z2[:1])
    c = tile_copy(1, 5, at_z(4), tile_in.at[3])
    c.start()
    sent.append(c)
    gather_tiles(z2[1:])
    c.wait_recv()
    tiles[2] = tiles[1] + tile_in[3] + tile_in[4] + tile_in[5]
    x1 = [(6 + i, at_x(d)) for i, d in enumerate(STEP4)]
    exchange(2, x1)

    for i, d in enumerate(STEP4):
        bulk[2 * i].wait_recv()
        pass_rows(block(row_f, (x + 4 - d) % 4), (x + 4 - d) % 4)
        bulk[2 * i + 1].wait_recv()
        pass_cols(block(col_f, (y + 4 - d) % 4), (y + 4 - d) % 4)

    gather_tiles(x1)
    tiles[3] = tiles[2] + tile_in[6] + tile_in[7] + tile_in[8]
    y1 = [(9 + i, at_y(d)) for i, d in enumerate(STEP4)]
    exchange(3, y1)
    gather_tiles(y1)
    tiles[4] = tiles[3] + tile_in[9] + tile_in[10] + tile_in[11]
    k1 = [(12, other)]
    exchange(4, k1)
    gather_tiles(k1)
    norm_squares = jnp.sum(tiles[4] + tile_in[12])
    factor = 0.6 * math.sqrt(ROWS) / (jnp.sqrt(jnp.full((8, 128), norm_squares, F32)) + 1e-07)
    factor = factor[0:1, 0:1]

    block(row_f, x)[...] = m_ref[...]
    block(col_f, y)[...] = m_ref[...]

    def scale(t, carry):
        at = pl.ds(pl.multiple_of(t * BLOCK, 16), BLOCK)
        row_b[at, :] = (row_f[at, :] * factor).astype(BF16)
        col_b[at, :] = (col_f[at, :] * factor).astype(BF16)
        return carry

    lax.fori_loop(0, 4, scale, 0)

    for t in range(2):
        send(m_ref, block(row_o, t), pass_s.at[0, t], pass_r.at[0, t], other).wait_recv()
    for t in range(4):
        send(m_ref, block(col_o, t), pass_s.at[1, t], pass_r.at[1, t], other).wait_recv()

    def scale_other(t, carry):
        at = pl.ds(pl.multiple_of(t * BLOCK, 16), BLOCK)
        col_ob[at, :] = (col_o[at, :] * factor).astype(BF16)
        return carry

    lax.fori_loop(0, 4, scale_other, 0)

    def scale_rows(t, carry):
        at = pl.ds(pl.multiple_of(t * BLOCK, 16), BLOCK)
        row_ob[at, :] = (row_o[at, :] * factor).astype(BF16)
        return carry

    lax.fori_loop(0, 2, scale_rows, 0)

    mine = pl.ds(pl.multiple_of(k * HALF, HALF), HALF)

    def gram_group(n, carry):
        at = pl.ds(pl.multiple_of(n * GROUP, GROUP), GROUP)
        total = rows_product(row_b[mine, :], col_b[at, :])
        total += rows_product(row_ob[...], col_ob[at, :])
        part[pl.ds(pl.multiple_of(n * HALF, HALF), HALF), :] = total
        return carry

    lax.fori_loop(0, GROUPS, gram_group, 0)

    def piece(c, p):
        return pl.ds(pl.multiple_of((c + 32) % 16 * CHUNK + PARTS[p][0], 16), PARTS[p][1])

    def inside(p):
        return pl.ds(PARTS[p][0], PARTS[p][1])

    def hop(d, s, p):
        ring = (ring_p, ring_m)[d]
        return send(
            ring.at[s, inside(p)], ring.at[s + 1, inside(p)],
            rs_s.at[d, s, p], rs_r.at[d, s, p], (at_z(1), at_z(15))[d],
        )

    for p in range(NP):
        ring_p[0, inside(p)] = part[piece(z + 8, p), :].astype(BF16)
        hop(0, 0, p).start()
        ring_m[0, inside(p)] = part[piece(z - 7, p), :].astype(BF16)
        hop(1, 0, p).start()

    def plus_step(s, p):
        hop(0, s - 1, p).wait_recv()
        ring_p[s, inside(p)] = (ring_p[s, inside(p)].astype(F32) + part[piece(z + 8 - s, p), :]).astype(BF16)
        hop(0, s, p).start()

    def minus_step(s, p):
        hop(1, s - 1, p).wait_recv()
        ring_m[s, inside(p)] = (ring_m[s, inside(p)].astype(F32) + part[piece(z - 7 + s, p), :]).astype(BF16)
        hop(1, s, p).start()

    def reduce_step(s, carry):
        for p in range(NP):
            plus_step(s, p)
            minus_step(s, p)
        return carry

    lax.fori_loop(1, 7, reduce_step, 0)
    for p in range(NP):
        plus_step(7, p)

    def onward(d, s, p):
        c = (z - s, z + s)[d]
        at = gram.at[k, piece(c, p)]
        return send(at, at, ag_s.at[d, s, p], ag_r.at[d, s, p], (at_z(1), at_z(15))[d])

    def arrived(d, s, p):
        c = (z - 1 - s, z + 1 + s)[d]
        at = gram.at[k, piece(c, p)]
        send(at, at, ag_s.at[d, s, p], ag_r.at[d, s, p], (at_z(1), at_z(15))[d]).wait_recv()

    def swap(slot, c, p):
        at = gram.at[k, piece(c, p)]
        return send(at, at, swap_s.at[slot, p], swap_r.at[slot, p], other)

    for p in range(NP):
        hop(0, 7, p).wait_recv()
        hop(1, 6, p).wait_recv()
        total = part[piece(z, p), :] + ring_p[8, inside(p)].astype(F32) + ring_m[7, inside(p)].astype(F32)
        gram[k, piece(z, p), :] = total.astype(BF16)
        onward(0, 0, p).start()
        onward(1, 0, p).start()
        swap(0, z, p).start()

    def gather_step(s, carry):
        for p in range(NP):
            arrived(0, s - 1, p)
            onward(0, s, p).start()
            swap(s, z - s, p).start()
            arrived(1, s - 1, p)
            onward(1, s, p).start()
            swap(8 + s, z + s, p).start()
        return carry

    lax.fori_loop(1, 7, gather_step, 0)
    for p in range(NP):
        arrived(0, 6, p)
        onward(0, 7, p).start()
        swap(7, z - 7, p).start()
        arrived(1, 6, p)
        swap(15, z + 7, p).start()
    for p in range(NP):
        arrived(0, 7, p)
        swap(8, z - 8, p).start()

    def swapped(s, carry):
        for p in range(NP):
            at = gram.at[1 - k, inside(p)]
            send(at, at, swap_s.at[s, p], swap_r.at[s, p], other).wait_recv()
        return carry

    lax.fori_loop(0, 16, swapped, 0)

    def times_gram(panel_0, panel_1, keep):
        @pl.when(k == 0)
        def _():
            def half(h, carry):
                total = jnp.zeros((HALF, WIDTH), F32)
                for n in range(GROUPS):
                    total += jnp.dot(
                        gram[h, n * HALF : (n + 1) * HALF, :],
                        panel_0[n * GROUP : (n + 1) * GROUP, :],
                        preferred_element_type=F32,
                    )
                at = pl.ds(pl.multiple_of(h * HALF, HALF), HALF)
                w[at, :] = total
                keep[at, :] = total.astype(BF16)
                return carry

            lax.fori_loop(0, 2, half, 0)

        @pl.when(k == 1)
        def _():
            def group(n, carry):
                total = jnp.zeros((GROUP, WIDTH), F32)
                for h in range(2):
                    total += columns_product(
                        gram[h, pl.ds(pl.multiple_of(n * HALF, HALF), HALF), :],
                        panel_1[h * HALF : (h + 1) * HALF, :],
                    )
                at = pl.ds(pl.multiple_of(n * GROUP, GROUP), GROUP)
                w[at, :] = total
                keep[at, :] = total.astype(BF16)
                return carry

            lax.fori_loop(0, GROUPS, group, 0)

    first = k == 0
    o_sum, o_all = jnp.where(first, x, y), jnp.where(first, y, x)

    def ring_sum(d):
        t = (o_sum + d) % 4
        return t, (jnp.where(first, y * 4 + t, t * 4 + x), col)

    def ring_all(d):
        t = (o_all + d) % 4
        return (jnp.where(first, t * 4 + x, y * 4 + t), col)

    def scatter(src, dst, ss, rs):
        copies = []
        for i, d in enumerate(STEP4):
            t, device = ring_sum(d)
            c = send(block(src, t), dst.at[i], ss.at[i], rs.at[i], device)
            c.start()
            sent.append(c)
            copies.append(c)
        total = block(w, o_sum)[...]
        for i, c in enumerate(copies):
            c.wait_recv()
            total += dst[i].astype(F32)
        return total

    times_gram(col_b, row_b, wb)
    y_own[...] = scatter(wb, y_in, ys_s, ys_r)
    block(y_all, o_all)[...] = y_own[...].astype(BF16)
    copies = []
    for i, d in enumerate(STEP4):
        c = send(block(y_all, o_all), block(y_all, o_all), yg_s.at[i], yg_r.at[i], ring_all(d))
        c.start()
        sent.append(c)
        copies.append(c)
    for c in copies:
        c.wait_recv()
    times_gram(y_all, y_all, wb2)
    z_own = scatter(wb2, z_in, zs_s, zs_r)
    scaled = block(row_b, x)[...].astype(F32)
    out_ref[...] = math.sqrt(COLS) * (quintic_a * scaled + (quintic_b * y_own[...] + quintic_c * z_own))

    for c in sent:
        c.wait_send()
    for t in range(2):
        send(block(row_o, t), block(row_o, t), pass_s.at[0, t], pass_r.at[0, t], other).wait_send()
    for t in range(4):
        send(block(col_o, t), block(col_o, t), pass_s.at[1, t], pass_r.at[1, t], other).wait_send()

    def left(s, carry):
        for p in range(NP):
            hop(0, s, p).wait_send()
            hop(1, s, p).wait_send()
            onward(0, s, p).wait_send()
            onward(1, s, p).wait_send()
            swap(s, z, p).wait_send()
            swap(8 + s, z, p).wait_send()
        return carry

    lax.fori_loop(0, 7, left, 0)
    for p in range(NP):
        hop(0, 7, p).wait_send()
        onward(0, 7, p).wait_send()
        swap(7, z, p).wait_send()
        swap(15, z, p).wait_send()


def body(momentum):
    dma = pltpu.SemaphoreType.DMA
    return pl.pallas_call(
        kernel,
        out_shape=jax.ShapeDtypeStruct((BLOCK, WIDTH), F32),
        in_specs=[pl.BlockSpec(memory_space=pltpu.VMEM)],
        out_specs=pl.BlockSpec(memory_space=pltpu.VMEM),
        scratch_shapes=[
            pltpu.VMEM((PANEL, WIDTH), F32),
            pltpu.VMEM((PANEL, WIDTH), F32),
            pltpu.VMEM((HALF, WIDTH), F32),
            pltpu.VMEM((PANEL, WIDTH), F32),
            pltpu.VMEM((PANEL, WIDTH), BF16),
            pltpu.VMEM((PANEL, WIDTH), BF16),
            pltpu.VMEM((HALF, WIDTH), BF16),
            pltpu.VMEM((PANEL, WIDTH), BF16),
            pltpu.VMEM((STACK, GROUP), F32),
            pltpu.VMEM((2, STACK, GROUP), BF16),
            pltpu.VMEM((9, CHUNK, GROUP), BF16),
            pltpu.VMEM((8, CHUNK, GROUP), BF16),
            pltpu.VMEM((5, 8, 128), F32),
            pltpu.VMEM((13, 8, 128), F32),
            pltpu.VMEM((PANEL, WIDTH), F32),
            pltpu.VMEM((PANEL, WIDTH), BF16),
            pltpu.VMEM((PANEL, WIDTH), BF16),
            pltpu.VMEM((PANEL, WIDTH), BF16),
            pltpu.VMEM((3, BLOCK, WIDTH), BF16),
            pltpu.VMEM((3, BLOCK, WIDTH), BF16),
            pltpu.VMEM((BLOCK, WIDTH), F32),
            dma((13,)), dma((13,)),
            dma((2, 3)), dma((2, 3)),
            dma((2, 4)), dma((2, 4)),
            dma((2, 8, NP)), dma((2, 8, NP)),
            dma((2, 8, NP)), dma((2, 8, NP)),
            dma((16, NP)), dma((16, NP)),
            dma((3,)), dma((3,)), dma((3,)), dma((3,)), dma((3,)), dma((3,)),
        ],
        compiler_params=pltpu.CompilerParams(
            collective_id=0, has_side_effects=True, vmem_limit_bytes=48 * 2**20
        ),
        name="muon",
    )(momentum)


def solution(mesh):
    return jax.shard_map(
        body, mesh=mesh, in_specs=(P("row", "col"),), out_specs=P("row", "col"), check_vma=False
    )
```

time: 608 us -> 120 us (0.20)
  waiting for transfers between devices: 457 us -> 0 us
  Pallas kernels: 0 us -> 118 us
  blocking collectives: 111 us -> 0 us
  between operations: 14.3 us -> 0.01 us
  matrix products: 13.9 us -> 0 us
  other arithmetic: 6.87 us -> 0 us
    all_gather x5 -> x0, waiting for transfers between devices: 339 us -> none  [the longest x1 76.3 us: body(): poly_panel = lax.all_gather(poly, 'col', axis=1, tiled=True)]
    pallas_call x0 -> x1, Pallas kernels: none -> 118 us  [body(): pl.pallas_call(kernel, out_shape=jax.ShapeDtypeStruct((BLOCK, WIDTH), F32...]
    psum x1 -> x0, waiting for transfers between devices: 118 us -> none  [from_root(): return lax.psum(jnp.where(mine, shard, jnp.zeros_like(shard)), axis)]
    psum x1 -> x0, blocking collectives: 111 us -> none  [body(): norm_squares = lax.psum(partial_sum, ('row', 'col'))]
    dot_general x3 -> x0, matrix products: 13.9 us -> none  [the longest x1 5.76 us: rows_product(): lax.dot_general(left, right, (((1,), (1,)), ((), ())), preferred_element_...]
  transfers between devices with their start and end apart: 6 -> 0, of which waited for: 6 -> 0; matrix products, arithmetic and copies ran while one was open for 1% -> 0% of each run, Pallas kernels for 0% -> 0%
where the time goes in v1:
time: 120 us; the launch traced here: 119 us
  Pallas kernels  118 us (98%)
  local copies, waits for them, and re-layouts  1.68 us (1%)
    pallas_call x1, Pallas kernels, body(): pl.pallas_call(kernel, out_shape=jax.ShapeDtypeStruct((BLOCK, WIDTH), F32...  118 us

profile of v1, /device:TPU:1, one launch (start us, length us, event | category | flops | bytes accessed | tf_op | source)
XLA Modules:
  0.0 119.5 jit_solution(10731881592438707676)
XLA Ops:
  0.0 0.0 copy-start
  0.0 1.0 copy-done
  1.0 117.8 %muon.1 = f32[288,256]{1,0:T(8,128)S(1)} custom-call(f32[288,256]{1,0:T(8,128)S(1)} %copy-done), custom_call_target="tpu_custom_call" | custom-call | tf_op jit(solution)/shard_map/muon/pallas_call | solution.py:397
  118.8 0.7 copy.3
Async XLA Ops:
  0.0 1.0 copy-start

commit v2 on v1

v2 whole, which is shorter than its diff:
```python
import functools
import math

import jax
import jax.numpy as jnp
from jax import lax
from jax.experimental import pallas as pl
from jax.experimental.pallas import tpu as pltpu
from jax.sharding import PartitionSpec as P

ROWS = 4608
COLS = 8192

quintic_a = 3.4445
quintic_b = -4.775
quintic_c = 2.0315

MESH = pl.DeviceIdType.MESH
F32 = jnp.float32
BF16 = jnp.bfloat16

BLOCK = 288
WIDTH = 256
PANEL = 4 * BLOCK
HALF = PANEL // 2
GROUP = 384
GROUPS = PANEL // GROUP
CHUNK = 112
STACK = 16 * CHUNK
PARTS = ((0, 64), (64, 48))
NP = len(PARTS)
STEP4 = (1, 3, 2)


def rows_product(left, right):
    return lax.dot_general(left, right, (((1,), (1,)), ((), ())), preferred_element_type=F32)


def columns_product(left, right):
    return lax.dot_general(left, right, (((0,), (0,)), ((), ())), preferred_element_type=F32)


def kernel(
    m_hbm,
    out_ref,
    m_ref, m_b, row_b, col_b, row_ob, col_ob, x_f, x_b,
    part, gram, ring_p, ring_m,
    tiles, tile_in,
    w, wb, wb2, y_all, y_in, z_in, y_own,
    load_s, tile_s, tile_r, bulk_s, bulk_r, pass_s, pass_r, wide_s, wide_r,
    rs_s, rs_r, ag_s, ag_r, swap_s, swap_r,
    ys_s, ys_r, yg_s, yg_r, zs_s, zs_r,
):
    row, col = lax.axis_index("row"), lax.axis_index("col")
    y, x, z, k = row // 4, row % 4, col // 2, col % 2
    first = k == 0

    def at_x(d):
        return (y * 4 + (x + d) % 4, col)

    def at_y(d):
        return (((y + d) % 4) * 4 + x, col)

    def at_z(d):
        return (row, ((z + d) % 16) * 2 + k)

    other = (row, z * 2 + 1 - k)

    o_sum, o_all = jnp.where(first, x, y), jnp.where(first, y, x)

    def ring_sum(d):
        t = (o_sum + d) % 4
        return t, (jnp.where(first, y * 4 + t, t * 4 + x), col)

    def ring_all(d):
        t = (o_all + d) % 4
        return (jnp.where(first, t * 4 + x, y * 4 + t), col)

    def send(src, dst, ss, rs, device):
        return pltpu.make_async_remote_copy(
            src_ref=src, dst_ref=dst, send_sem=ss, recv_sem=rs, device_id=device, device_id_type=MESH
        )

    sent = []

    def start(src, dst, ss, rs, device):
        c = send(src, dst, ss, rs, device)
        c.start()
        sent.append(c)
        return c

    load = pltpu.make_async_copy(m_hbm, m_ref, load_s)
    load.start()
    barrier = pltpu.get_barrier_semaphore()
    peers = [at_x(d) for d in STEP4] + [at_y(d) for d in STEP4] + [other]
    peers += [at_z(d) for d in (1, 15, 2, 14)]
    for peer in peers:
        pl.semaphore_signal(barrier, inc=1, device_id=peer, device_id_type=MESH)
    load.wait()

    def block(ref, t, rows=BLOCK):
        return ref.at[pl.ds(pl.multiple_of(t * rows, 16), rows), :]

    m_b[...] = m_ref[...].astype(BF16)
    squares = m_ref[...] * m_ref[...]
    squares = jnp.sum(squares.reshape(BLOCK // 8, 8, WIDTH), axis=0)
    tiles[0] = squares[:, :128] + squares[:, 128:]

    pl.semaphore_wait(barrier, len(peers))

    bulk = []
    for i, d in enumerate(STEP4):
        bulk.append(start(m_b, block(row_b, x), bulk_s.at[0, i], bulk_r.at[0, i], at_x(d)))
        bulk.append(start(m_b, block(col_b, y), bulk_s.at[1, i], bulk_r.at[1, i], at_y(d)))

    def pass_rows(src, t):
        @pl.when(t // 2 != k)
        def _():
            send(src, block(row_ob, t % 2), pass_s.at[0, t % 2], pass_r.at[0, t % 2], other).start()

    def pass_cols(src, t):
        send(src, block(col_ob, t), pass_s.at[1, t], pass_r.at[1, t], other).start()

    pass_rows(m_b, x)
    pass_cols(m_b, y)

    def exchange(stage, slots):
        for slot, device in slots:
            start(tiles.at[stage], tile_in.at[slot], tile_s.at[slot], tile_r.at[slot], device)

    def gathered(stage, slots):
        total = tiles[stage]
        for slot, device in slots:
            send(tiles.at[0], tile_in.at[slot], tile_s.at[slot], tile_r.at[slot], device).wait_recv()
            total += tile_in[slot]
        tiles[stage + 1] = total

    near = [(0, at_z(1)), (1, at_z(15)), (2, at_z(2))]
    far = [(3, at_z(4)), (4, at_z(12))]
    along_x = [(6 + i, at_x(d)) for i, d in enumerate(STEP4)]
    along_y = [(9 + i, at_y(d)) for i, d in enumerate(STEP4)]
    exchange(0, near)

    block(row_b, x)[...] = m_b[...]
    block(col_b, y)[...] = m_b[...]
    block(x_f, o_all)[...] = m_ref[...]
    part[STACK - 64 : STACK, :] = jnp.zeros((64, GROUP), F32)

    for i, d in enumerate(STEP4):
        bulk[2 * i].wait_recv()
        pass_rows(block(row_b, (x + 4 - d) % 4), (x + 4 - d) % 4)
        bulk[2 * i + 1].wait_recv()
        pass_cols(block(col_b, (y + 4 - d) % 4), (y + 4 - d) % 4)

    wide = [
        start(m_ref, block(x_f, o_all), wide_s.at[i], wide_r.at[i], ring_all(d)) for i, d in enumerate(STEP4)
    ]

    mine = pl.ds(pl.multiple_of(k * HALF, HALF), HALF)

    def gram_own(n, carry):
        at = pl.ds(pl.multiple_of(n * GROUP, GROUP), GROUP)
        part[pl.ds(pl.multiple_of(n * HALF, HALF), HALF), :] = rows_product(row_b[mine, :], col_b[at, :])
        return carry

    lax.fori_loop(0, GROUPS, gram_own, 0)
    for t in range(2):
        send(m_b, block(row_ob, t), pass_s.at[0, t], pass_r.at[0, t], other).wait_recv()
    for t in range(4):
        send(m_b, block(col_ob, t), pass_s.at[1, t], pass_r.at[1, t], other).wait_recv()

    def gram_other(n, carry):
        at = pl.ds(pl.multiple_of(n * GROUP, GROUP), GROUP)
        part[pl.ds(pl.multiple_of(n * HALF, HALF), HALF), :] += rows_product(row_ob[...], col_ob[at, :])
        return carry

    lax.fori_loop(0, GROUPS, gram_other, 0)

    def piece(c, p):
        return pl.ds(pl.multiple_of((c + 32) % 16 * CHUNK + PARTS[p][0], 16), PARTS[p][1])

    def inside(p):
        return pl.ds(PARTS[p][0], PARTS[p][1])

    def hop(d, s, p):
        ring = (ring_p, ring_m)[d]
        return send(
            ring.at[s, inside(p)], ring.at[s + 1, inside(p)],
            rs_s.at[d, s, p], rs_r.at[d, s, p], (at_z(1), at_z(15))[d],
        )

    for p in range(NP):
        ring_p[0, inside(p)] = part[piece(z + 8, p), :].astype(BF16)
        hop(0, 0, p).start()
        ring_m[0, inside(p)] = part[piece(z - 7, p), :].astype(BF16)
        hop(1, 0, p).start()

    def plus_step(s, p):
        hop(0, s - 1, p).wait_recv()
        ring_p[s, inside(p)] = (ring_p[s, inside(p)].astype(F32) + part[piece(z + 8 - s, p), :]).astype(BF16)
        hop(0, s, p).start()

    def minus_step(s, p):
        hop(1, s - 1, p).wait_recv()
        ring_m[s, inside(p)] = (ring_m[s, inside(p)].astype(F32) + part[piece(z - 7 + s, p), :]).astype(BF16)
        hop(1, s, p).start()

    def reduce_step(s, carry):
        for p in range(NP):
            plus_step(s, p)
            minus_step(s, p)
        return carry

    gathered(0, near)
    lax.fori_loop(1, 4, reduce_step, 0)
    exchange(1, far)
    lax.fori_loop(4, 6, reduce_step, 0)
    send(tiles.at[1], tile_in.at[3], tile_s.at[3], tile_r.at[3], at_z(4)).wait_recv()
    onward_tile = start(tile_in.at[3], tile_in.at[5], tile_s.at[5], tile_r.at[5], at_z(4))
    lax.fori_loop(6, 7, reduce_step, 0)
    for p in range(NP):
        plus_step(7, p)
    send(tiles.at[1], tile_in.at[4], tile_s.at[4], tile_r.at[4], at_z(12)).wait_recv()
    onward_tile.wait_recv()
    tiles[2] = tiles[1] + tile_in[3] + tile_in[4] + tile_in[5]
    exchange(2, along_x)

    def onward(d, s, p):
        at = gram.at[k, piece((z - s, z + s)[d], p)]
        return send(at, at, ag_s.at[d, s, p], ag_r.at[d, s, p], (at_z(1), at_z(15))[d])

    def arrived(d, s, p):
        at = gram.at[k, piece((z - s, z + s)[d], p)]
        send(at, at, ag_s.at[d, s - 1, p], ag_r.at[d, s - 1, p], (at_z(1), at_z(15))[d]).wait_recv()

    def swap(slot, c, p):
        at = gram.at[k, piece(c, p)]
        return send(at, at, swap_s.at[slot, p], swap_r.at[slot, p], other)

    for p in range(NP):
        hop(0, 7, p).wait_recv()
        hop(1, 6, p).wait_recv()
        total = part[piece(z, p), :] + ring_p[8, inside(p)].astype(F32) + ring_m[7, inside(p)].astype(F32)
        gram[k, piece(z, p), :] = total.astype(BF16)
        onward(0, 0, p).start()
        onward(1, 0, p).start()
    for p in range(NP):
        swap(0, z, p).start()

    def gather_step(s, carry):
        for p in range(NP):
            arrived(0, s, p)
            onward(0, s, p).start()
            arrived(1, s, p)
            onward(1, s, p).start()
        for p in range(NP):
            swap(s, z - s, p).start()
            swap(8 + s, z + s, p).start()
        return carry

    lax.fori_loop(1, 3, gather_step, 0)
    gathered(2, along_x)
    exchange(3, along_y)
    lax.fori_loop(3, 5, gather_step, 0)
    gathered(3, along_y)
    exchange(4, [(12, other)])
    lax.fori_loop(5, 6, gather_step, 0)
    gathered(4, [(12, other)])
    norm_squares = jnp.sum(tiles[5])
    factor = 0.6 * math.sqrt(ROWS) / (jnp.sqrt(jnp.full((8, 128), norm_squares, F32)) + 1e-07)
    factor = factor[0:1, 0:1]
    lax.fori_loop(6, 7, gather_step, 0)

    for c in wide:
        c.wait_recv()

    def scale(t, carry):
        at = pl.ds(pl.multiple_of(t * BLOCK, 16), BLOCK)
        x_b[at, :] = (x_f[at, :] * factor).astype(BF16)
        return carry

    lax.fori_loop(0, 4, scale, 0)

    for p in range(NP):
        arrived(0, 7, p)
        onward(0, 7, p).start()
        arrived(1, 7, p)
    for p in range(NP):
        swap(7, z - 7, p).start()
        swap(15, z + 7, p).start()
    for p in range(NP):
        arrived(0, 8, p)
        swap(8, z - 8, p).start()

    def swapped(s, carry):
        for p in range(NP):
            at = gram.at[1 - k, inside(p)]
            send(at, at, swap_s.at[s, p], swap_r.at[s, p], other).wait_recv()
        return carry

    lax.fori_loop(0, 16, swapped, 0)

    squared_factor = factor * factor

    def times_gram(panel, keep):
        @pl.when(first)
        def _():
            def half(h, carry):
                total = jnp.zeros((HALF, WIDTH), F32)
                for n in range(GROUPS):
                    total += jnp.dot(
                        gram[h, n * HALF : (n + 1) * HALF, :],
                        panel[n * GROUP : (n + 1) * GROUP, :],
                        preferred_element_type=F32,
                    )
                at = pl.ds(pl.multiple_of(h * HALF, HALF), HALF)
                total = total * squared_factor
                w[at, :] = total
                keep[at, :] = total.astype(BF16)
                return carry

            lax.fori_loop(0, 2, half, 0)

        @pl.when(k == 1)
        def _():
            def group(n, carry):
                total = jnp.zeros((GROUP, WIDTH), F32)
                for h in range(2):
                    total += columns_product(
                        gram[h, pl.ds(pl.multiple_of(n * HALF, HALF), HALF), :],
                        panel[h * HALF : (h + 1) * HALF, :],
                    )
                at = pl.ds(pl.multiple_of(n * GROUP, GROUP), GROUP)
                total = total * squared_factor
                w[at, :] = total
                keep[at, :] = total.astype(BF16)
                return carry

            lax.fori_loop(0, GROUPS, group, 0)

    def scatter(src, dst, ss, rs):
        copies = []
        for i, d in enumerate(STEP4):
            t, device = ring_sum(d)
            copies.append(start(block(src, t), dst.at[i], ss.at[i], rs.at[i], device))
        total = block(w, o_sum)[...]
        for i, c in enumerate(copies):
            c.wait_recv()
            total += dst[i].astype(F32)
        return total

    times_gram(x_b, wb)
    y_own[...] = scatter(wb, y_in, ys_s, ys_r)
    block(y_all, o_all)[...] = y_own[...].astype(BF16)
    copies = [
        start(block(y_all, o_all), block(y_all, o_all), yg_s.at[i], yg_r.at[i], ring_all(d))
        for i, d in enumerate(STEP4)
    ]
    for c in copies:
        c.wait_recv()
    times_gram(y_all, wb2)
    z_own = scatter(wb2, z_in, zs_s, zs_r)
    scaled = block(x_b, o_all)[...].astype(F32)
    out_ref[...] = math.sqrt(COLS) * (quintic_a * scaled + (quintic_b * y_own[...] + quintic_c * z_own))

    for c in sent:
        c.wait_send()
    for t in range(2):
        send(block(row_ob, t), block(row_ob, t), pass_s.at[0, t], pass_r.at[0, t], other).wait_send()
    for t in range(4):
        send(block(col_ob, t), block(col_ob, t), pass_s.at[1, t], pass_r.at[1, t], other).wait_send()

    def left(s, carry):
        for p in range(NP):
            hop(0, s, p).wait_send()
            hop(1, s, p).wait_send()
            onward(0, s, p).wait_send()
            onward(1, s, p).wait_send()
            swap(s, z, p).wait_send()
            swap(8 + s, z, p).wait_send()
        return carry

    lax.fori_loop(0, 7, left, 0)
    for p in range(NP):
        hop(0, 7, p).wait_send()
        onward(0, 7, p).wait_send()
        swap(7, z, p).wait_send()
        swap(15, z, p).wait_send()


def body(momentum):
    dma = pltpu.SemaphoreType.DMA
    return pl.pallas_call(
        kernel,
        out_shape=jax.ShapeDtypeStruct((BLOCK, WIDTH), F32),
        in_specs=[pl.BlockSpec(memory_space=pltpu.HBM)],
        out_specs=pl.BlockSpec(memory_space=pltpu.VMEM),
        scratch_shapes=[
            pltpu.VMEM((BLOCK, WIDTH), F32),
            pltpu.VMEM((BLOCK, WIDTH), BF16),
            pltpu.VMEM((PANEL, WIDTH), BF16),
            pltpu.VMEM((PANEL, WIDTH), BF16),
            pltpu.VMEM((HALF, WIDTH), BF16),
            pltpu.VMEM((PANEL, WIDTH), BF16),
            pltpu.VMEM((PANEL, WIDTH), F32),
            pltpu.VMEM((PANEL, WIDTH), BF16),
            pltpu.VMEM((STACK, GROUP), F32),
            pltpu.VMEM((2, STACK, GROUP), BF16),
            pltpu.VMEM((9, CHUNK, GROUP), BF16),
            pltpu.VMEM((8, CHUNK, GROUP), BF16),
            pltpu.VMEM((6, 8, 128), F32),
            pltpu.VMEM((13, 8, 128), F32),
            pltpu.VMEM((PANEL, WIDTH), F32),
            pltpu.VMEM((PANEL, WIDTH), BF16),
            pltpu.VMEM((PANEL, WIDTH), BF16),
            pltpu.VMEM((PANEL, WIDTH), BF16),
            pltpu.VMEM((3, BLOCK, WIDTH), BF16),
            pltpu.VMEM((3, BLOCK, WIDTH), BF16),
            pltpu.VMEM((BLOCK, WIDTH), F32),
            dma, dma((13,)), dma((13,)),
            dma((2, 3)), dma((2, 3)),
            dma((2, 4)), dma((2, 4)),
            dma((3,)), dma((3,)),
            dma((2, 8, NP)), dma((2, 8, NP)),
            dma((2, 8, NP)), dma((2, 8, NP)),
            dma((16, NP)), dma((16, NP)),
            dma((3,)), dma((3,)), dma((3,)), dma((3,)), dma((3,)), dma((3,)),
        ],
        compiler_params=pltpu.CompilerParams(
            collective_id=0, has_side_effects=True, vmem_limit_bytes=48 * 2**20
        ),
        name="muon",
    )(momentum)


def solution(mesh):
    return jax.shard_map(
        body, mesh=mesh, in_specs=(P("row", "col"),), out_specs=P("row", "col"), check_vma=False
    )
```

time: 120 us -> 108 us (0.900)
  Pallas kernels: 118 us -> 106 us
    pallas_call x1, Pallas kernels: 118 us -> 106 us  [body(): pl.pallas_call(kernel, out_shape=jax.ShapeDtypeStruct((BLOCK, WIDTH), F32...]
where the time goes in v2:
time: 108 us
  Pallas kernels  106 us (98%)
  local copies, waits for them, and re-layouts  1.68 us (2%)
    pallas_call x1, Pallas kernels, body(): pl.pallas_call(kernel, out_shape=jax.ShapeDtypeStruct((BLOCK, WIDTH), F32...  106 us

profile of v2, /device:TPU:1, one launch (start us, length us, event | category | flops | bytes accessed | tf_op | source)
XLA Modules:
  0.0 108.1 jit_solution(6172492508920062139)
XLA Ops:
  0.0 0.0 copy-start
  0.0 1.0 copy-done
  1.0 106.4 %muon.1 = f32[288,256]{1,0:T(8,128)S(1)} custom-call(f32[288,256]{1,0:T(8,128)S(1)} %copy-done), custom_call_target="tpu_custom_call" | custom-call | tf_op jit(solution)/shard_map/muon/pallas_call | solution.py:393
  107.4 0.7 copy.3
Async XLA Ops:
  0.0 1.0 copy-start

commit v3 on v2

--- a/solution.py
+++ b/solution.py
@@ -27,8 +27,9 @@
 GROUPS = PANEL // GROUP
 CHUNK = 112
 STACK = 16 * CHUNK
-PARTS = ((0, 64), (64, 48))
+PARTS = ((0, 32), (32, 32), (64, 32), (96, 16))
 NP = len(PARTS)
+SIDE = WIDTH // 2
 STEP4 = (1, 3, 2)
 
 
@@ -41,13 +42,13 @@
 
 
 def kernel(
-    m_hbm,
+    m_ref,
     out_ref,
-    m_ref, m_b, row_b, col_b, row_ob, col_ob, x_f, x_b,
+    m_b, row_b, col_b, row_ob, col_ob, x_f, x_b,
     part, gram, ring_p, ring_m,
     tiles, tile_in,
     w, wb, wb2, y_all, y_in, z_in, y_own,
-    load_s, tile_s, tile_r, bulk_s, bulk_r, pass_s, pass_r, wide_s, wide_r,
+    tile_s, tile_r, bulk_s, bulk_r, pass_s, pass_r, wide_s, wide_r,
     rs_s, rs_r, ag_s, ag_r, swap_s, swap_r,
     ys_s, ys_r, yg_s, yg_r, zs_s, zs_r,
 ):
@@ -89,14 +90,11 @@
         sent.append(c)
         return c
 
-    load = pltpu.make_async_copy(m_hbm, m_ref, load_s)
-    load.start()
     barrier = pltpu.get_barrier_semaphore()
     peers = [at_x(d) for d in STEP4] + [at_y(d) for d in STEP4] + [other]
     peers += [at_z(d) for d in (1, 15, 2, 14)]
     for peer in peers:
         pl.semaphore_signal(barrier, inc=1, device_id=peer, device_id_type=MESH)
-    load.wait()
 
     def block(ref, t, rows=BLOCK):
         return ref.at[pl.ds(pl.multiple_of(t * rows, 16), rows), :]
@@ -189,11 +187,19 @@
             rs_s.at[d, s, p], rs_r.at[d, s, p], (at_z(1), at_z(15))[d],
         )
 
+    def jump(p):
+        return send(
+            ring_p.at[0, inside(p)], ring_p.at[9, inside(p)], rs_s.at[0, 0, p], rs_r.at[0, 0, p], at_z(2)
+        )
+
     for p in range(NP):
         ring_p[0, inside(p)] = part[piece(z + 8, p), :].astype(BF16)
-        hop(0, 0, p).start()
+        jump(p).start()
         ring_m[0, inside(p)] = part[piece(z - 7, p), :].astype(BF16)
         hop(1, 0, p).start()
+    for p in range(NP):
+        ring_p[1, inside(p)] = part[piece(z + 7, p), :].astype(BF16)
+        hop(0, 1, p).start()
 
     def plus_step(s, p):
         hop(0, s - 1, p).wait_recv()
@@ -212,7 +218,16 @@
         return carry
 
     gathered(0, near)
-    lax.fori_loop(1, 4, reduce_step, 0)
+    for p in range(NP):
+        minus_step(1, p)
+    for p in range(NP):
+        jump(p).wait_recv()
+        hop(0, 1, p).wait_recv()
+        total = ring_p[2, inside(p)].astype(F32) + ring_p[9, inside(p)].astype(F32) + part[piece(z + 6, p), :]
+        ring_p[2, inside(p)] = total.astype(BF16)
+        hop(0, 2, p).start()
+        minus_step(2, p)
+    lax.fori_loop(3, 4, reduce_step, 0)
     exchange(1, far)
     lax.fori_loop(4, 6, reduce_step, 0)
     send(tiles.at[1], tile_in.at[3], tile_s.at[3], tile_r.at[3], at_z(4)).wait_recv()
@@ -233,9 +248,16 @@
         at = gram.at[k, piece((z - s, z + s)[d], p)]
         send(at, at, ag_s.at[d, s - 1, p], ag_r.at[d, s - 1, p], (at_z(1), at_z(15))[d]).wait_recv()
 
-    def swap(slot, c, p):
-        at = gram.at[k, piece(c, p)]
-        return send(at, at, swap_s.at[slot, p], swap_r.at[slot, p], other)
+    def chunk(c):
+        return pl.ds(pl.multiple_of((c + 32) % 16 * CHUNK, 16), CHUNK)
+
+    def swap(slot, c):
+        at = gram.at[k, chunk(c)]
+        return send(at, at, swap_s.at[slot], swap_r.at[slot], other)
+
+    def swapped(slot):
+        at = gram.at[1 - k, 0:CHUNK]
+        send(at, at, swap_s.at[slot], swap_r.at[slot], other).wait_recv()
 
     for p in range(NP):
         hop(0, 7, p).wait_recv()
@@ -244,8 +266,7 @@
         gram[k, piece(z, p), :] = total.astype(BF16)
         onward(0, 0, p).start()
         onward(1, 0, p).start()
-    for p in range(NP):
-        swap(0, z, p).start()
+    swap(0, z).start()
 
     def gather_step(s, carry):
         for p in range(NP):
@@ -253,9 +274,8 @@
             onward(0, s, p).start()
             arrived(1, s, p)
             onward(1, s, p).start()
-        for p in range(NP):
-            swap(s, z - s, p).start()
-            swap(8 + s, z + s, p).start()
+        swap(s, z - s).start()
+        swap(8 + s, z + s).start()
         return carry
 
     lax.fori_loop(1, 3, gather_step, 0)
@@ -269,54 +289,58 @@
     norm_squares = jnp.sum(tiles[5])
     factor = 0.6 * math.sqrt(ROWS) / (jnp.sqrt(jnp.full((8, 128), norm_squares, F32)) + 1e-07)
     factor = factor[0:1, 0:1]
-    lax.fori_loop(6, 7, gather_step, 0)
+    for p in range(NP):
+        arrived(0, 6, p)
+        at = gram.at[k, piece(z - 6, p)]
+        send(at, at, ag_s.at[0, 7, p], ag_r.at[0, 7, p], at_z(2)).start()
+        onward(0, 6, p).start()
+        arrived(1, 6, p)
+        onward(1, 6, p).start()
+    swap(6, z - 6).start()
+    swap(14, z + 6).start()
 
     for c in wide:
         c.wait_recv()
 
     def scale(t, carry):
         at = pl.ds(pl.multiple_of(t * BLOCK, 16), BLOCK)
-        x_b[at, :] = (x_f[at, :] * factor).astype(BF16)
+        rounded = (x_f[at, :] * factor).astype(BF16)
+        x_b[0, at, :] = rounded[:, :SIDE]
+        x_b[1, at, :] = rounded[:, SIDE:]
         return carry
 
     lax.fori_loop(0, 4, scale, 0)
 
     for p in range(NP):
         arrived(0, 7, p)
-        onward(0, 7, p).start()
         arrived(1, 7, p)
-    for p in range(NP):
-        swap(7, z - 7, p).start()
-        swap(15, z + 7, p).start()
+    swap(7, z - 7).start()
+    swap(15, z + 7).start()
+    for slot in (0, 1, 2, 3, 4, 5, 6, 9, 10, 11, 12, 13, 14):
+        swapped(slot)
     for p in range(NP):
         arrived(0, 8, p)
-        swap(8, z - 8, p).start()
-
-    def swapped(s, carry):
-        for p in range(NP):
-            at = gram.at[1 - k, inside(p)]
-            send(at, at, swap_s.at[s, p], swap_r.at[s, p], other).wait_recv()
-        return carry
-
-    lax.fori_loop(0, 16, swapped, 0)
+    swap(8, z - 8).start()
+    for slot in (7, 15, 8):
+        swapped(slot)
 
     squared_factor = factor * factor
 
-    def times_gram(panel, keep):
+    def times_gram(panel, keep, c):
         @pl.when(first)
         def _():
             def half(h, carry):
-                total = jnp.zeros((HALF, WIDTH), F32)
+                total = jnp.zeros((HALF, SIDE), F32)
                 for n in range(GROUPS):
                     total += jnp.dot(
                         gram[h, n * HALF : (n + 1) * HALF, :],
-                        panel[n * GROUP : (n + 1) * GROUP, :],
+                        panel[c, n * GROUP : (n + 1) * GROUP, :],
                         preferred_element_type=F32,
                     )
                 at = pl.ds(pl.multiple_of(h * HALF, HALF), HALF)
                 total = total * squared_factor
-                w[at, :] = total
-                keep[at, :] = total.astype(BF16)
+                w[c, at, :] = total
+                keep[c, at, :] = total.astype(BF16)
                 return carry
 
             lax.fori_loop(0, 2, half, 0)
@@ -324,44 +348,82 @@
         @pl.when(k == 1)
         def _():
             def group(n, carry):
-                total = jnp.zeros((GROUP, WIDTH), F32)
+                total = jnp.zeros((GROUP, SIDE), F32)
                 for h in range(2):
                     total += columns_product(
                         gram[h, pl.ds(pl.multiple_of(n * HALF, HALF), HALF), :],
-                        panel[h * HALF : (h + 1) * HALF, :],
+                        panel[c, h * HALF : (h + 1) * HALF, :],
                     )
                 at = pl.ds(pl.multiple_of(n * GROUP, GROUP), GROUP)
                 total = total * squared_factor
-                w[at, :] = total
-                keep[at, :] = total.astype(BF16)
+                w[c, at, :] = total
+                keep[c, at, :] = total.astype(BF16)
                 return carry
 
             lax.fori_loop(0, GROUPS, group, 0)
 
-    def scatter(src, dst, ss, rs):
+    def side(ref, c, t):
+        return ref.at[c, pl.ds(pl.multiple_of(t * BLOCK, 16), BLOCK), :]
+
+    def scatter(src, dst, ss, rs, c):
         copies = []
         for i, d in enumerate(STEP4):
             t, device = ring_sum(d)
-            copies.append(start(block(src, t), dst.at[i], ss.at[i], rs.at[i], device))
-        total = block(w, o_sum)[...]
-        for i, c in enumerate(copies):
-            c.wait_recv()
-            total += dst[i].astype(F32)
+            copies.append(send(side(src, c, t), dst.at[c, i], ss.at[c, i], rs.at[c, i], device))
+            copies[-1].start()
+        return copies
+
+    def summed(copies, dst, c):
+        total = side(w, c, o_sum)[...]
+        for i, copy in enumerate(copies):
+            copy.wait_recv()
+            total += dst[c, i].astype(F32)
         return total
 
-    times_gram(x_b, wb)
-    y_own[...] = scatter(wb, y_in, ys_s, ys_r)
-    block(y_all, o_all)[...] = y_own[...].astype(BF16)
-    copies = [
-        start(block(y_all, o_all), block(y_all, o_all), yg_s.at[i], yg_r.at[i], ring_all(d))
-        for i, d in enumerate(STEP4)
-    ]
-    for c in copies:
-        c.wait_recv()
-    times_gram(y_all, wb2)
-    z_own = scatter(wb2, z_in, zs_s, zs_r)
-    scaled = block(x_b, o_all)[...].astype(F32)
-    out_ref[...] = math.sqrt(COLS) * (quintic_a * scaled + (quintic_b * y_own[...] + quintic_c * z_own))
+    y_sum = []
+    for c in range(2):
+        times_gram(x_b, wb, c)
+        y_sum.append(scatter(wb, y_in, ys_s, ys_r, c))
+
+    def left(s, carry):
+        for p in range(NP):
+            hop(0, s, p).wait_send()
+            hop(1, s, p).wait_send()
+        return carry
+
+    lax.fori_loop(0, 7, left, 0)
+    for p in range(NP):
+        hop(0, 7, p).wait_send()
+
+    y_gather = []
+    for c in range(2):
+        total = summed(y_sum[c], y_in, c)
+        y_own[c] = total
+        side(y_all, c, o_all)[...] = total.astype(BF16)
+        copies = []
+        for i, d in enumerate(STEP4):
+            copies.append(
+                send(side(y_all, c, o_all), side(y_all, c, o_all), yg_s.at[c, i], yg_r.at[c, i], ring_all(d))
+            )
+            copies[-1].start()
+        y_gather.append(copies)
+
+    def left_too(s, carry):
+        for p in range(NP):
+            onward(0, s, p).wait_send()
+            onward(1, s, p).wait_send()
+        return carry
+
+    lax.fori_loop(0, 7, left_too, 0)
+    for p in range(NP):
+        onward(0, 7, p).wait_send()
+
+    z_sum = []
+    for c in range(2):
+        for copy in y_gather[c]:
+            copy.wait_recv()
+        times_gram(y_all, wb2, c)
+        z_sum.append(scatter(wb2, z_in, zs_s, zs_r, c))
 
     for c in sent:
         c.wait_send()
@@ -369,23 +431,20 @@
         send(block(row_ob, t), block(row_ob, t), pass_s.at[0, t], pass_r.at[0, t], other).wait_send()
     for t in range(4):
         send(block(col_ob, t), block(col_ob, t), pass_s.at[1, t], pass_r.at[1, t], other).wait_send()
-
-    def left(s, carry):
-        for p in range(NP):
-            hop(0, s, p).wait_send()
-            hop(1, s, p).wait_send()
-            onward(0, s, p).wait_send()
-            onward(1, s, p).wait_send()
-            swap(s, z, p).wait_send()
-            swap(8 + s, z, p).wait_send()
-        return carry
-
-    lax.fori_loop(0, 7, left, 0)
-    for p in range(NP):
-        hop(0, 7, p).wait_send()
-        onward(0, 7, p).wait_send()
-        swap(7, z, p).wait_send()
-        swap(15, z, p).wait_send()
+    for slot in range(16):
+        swap(slot, z).wait_send()
+    for copies in y_sum + y_gather:
+        for copy in copies:
+            copy.wait_send()
+
+    for c in range(2):
+        z_own = summed(z_sum[c], z_in, c)
+        scaled = side(x_b, c, o_all)[...].astype(F32)
+        total = quintic_b * y_own[c] + quintic_c * z_own
+        out_ref[:, c * SIDE : (c + 1) * SIDE] = math.sqrt(COLS) * (quintic_a * scaled + total)
+    for copies in z_sum:
+        for copy in copies:
+            copy.wait_send()
 
 
 def body(momentum):
@@ -393,38 +452,37 @@
     return pl.pallas_call(
         kernel,
         out_shape=jax.ShapeDtypeStruct((BLOCK, WIDTH), F32),
-        in_specs=[pl.BlockSpec(memory_space=pltpu.HBM)],
+        in_specs=[pl.BlockSpec(memory_space=pltpu.VMEM)],
         out_specs=pl.BlockSpec(memory_space=pltpu.VMEM),
         scratch_shapes=[
-            pltpu.VMEM((BLOCK, WIDTH), F32),
             pltpu.VMEM((BLOCK, WIDTH), BF16),
             pltpu.VMEM((PANEL, WIDTH), BF16),
             pltpu.VMEM((PANEL, WIDTH), BF16),
             pltpu.VMEM((HALF, WIDTH), BF16),
             pltpu.VMEM((PANEL, WIDTH), BF16),
             pltpu.VMEM((PANEL, WIDTH), F32),
-            pltpu.VMEM((PANEL, WIDTH), BF16),
+            pltpu.VMEM((2, PANEL, SIDE), BF16),
             pltpu.VMEM((STACK, GROUP), F32),
             pltpu.VMEM((2, STACK, GROUP), BF16),
-            pltpu.VMEM((9, CHUNK, GROUP), BF16),
+            pltpu.VMEM((10, CHUNK, GROUP), BF16),
             pltpu.VMEM((8, CHUNK, GROUP), BF16),
             pltpu.VMEM((6, 8, 128), F32),
             pltpu.VMEM((13, 8, 128), F32),
-            pltpu.VMEM((PANEL, WIDTH), F32),
-            pltpu.VMEM((PANEL, WIDTH), BF16),
-            pltpu.VMEM((PANEL, WIDTH), BF16),
-            pltpu.VMEM((PANEL, WIDTH), BF16),
-            pltpu.VMEM((3, BLOCK, WIDTH), BF16),
-            pltpu.VMEM((3, BLOCK, WIDTH), BF16),
-            pltpu.VMEM((BLOCK, WIDTH), F32),
-            dma, dma((13,)), dma((13,)),
+            pltpu.VMEM((2, PANEL, SIDE), F32),
+            pltpu.VMEM((2, PANEL, SIDE), BF16),
+            pltpu.VMEM((2, PANEL, SIDE), BF16),
+            pltpu.VMEM((2, PANEL, SIDE), BF16),
+            pltpu.VMEM((2, 3, BLOCK, SIDE), BF16),
+            pltpu.VMEM((2, 3, BLOCK, SIDE), BF16),
+            pltpu.VMEM((2, BLOCK, SIDE), F32),
+            dma((13,)), dma((13,)),
             dma((2, 3)), dma((2, 3)),
             dma((2, 4)), dma((2, 4)),
             dma((3,)), dma((3,)),
             dma((2, 8, NP)), dma((2, 8, NP)),
             dma((2, 8, NP)), dma((2, 8, NP)),
-            dma((16, NP)), dma((16, NP)),
-            dma((3,)), dma((3,)), dma((3,)), dma((3,)), dma((3,)), dma((3,)),
+            dma((16,)), dma((16,)),
+            dma((2, 3)), dma((2, 3)), dma((2, 3)), dma((2, 3)), dma((2, 3)), dma((2, 3)),
         ],
         compiler_params=pltpu.CompilerParams(
             collective_id=0, has_side_effects=True, vmem_limit_bytes=48 * 2**20

time: 108 us -> 100 us (0.926)
  Pallas kernels: 106 us -> 98.2 us
    pallas_call x1, Pallas kernels: 106 us -> 98.2 us  [body(): pl.pallas_call(kernel, out_shape=jax.ShapeDtypeStruct((BLOCK, WIDTH), F32...]
where the time goes in v3:
time: 100 us; the launch traced here: 99.9 us
  Pallas kernels  98.2 us (98%)
  local copies, waits for them, and re-layouts  1.68 us (2%)
    pallas_call x1, Pallas kernels, body(): pl.pallas_call(kernel, out_shape=jax.ShapeDtypeStruct((BLOCK, WIDTH), F32...  98.2 us

profile of v3, /device:TPU:1, one launch (start us, length us, event | category | flops | bytes accessed | tf_op | source)
XLA Modules:
  0.0 99.9 jit_solution(11891830273851923086)
XLA Ops:
  0.0 0.0 copy-start
  0.0 1.0 copy-done
  1.0 98.2 %muon.1 = f32[288,256]{1,0:T(8,128)S(1)} custom-call(f32[288,256]{1,0:T(8,128)S(1)} %copy-done), custom_call_target="tpu_custom_call" | custom-call | tf_op jit(solution)/shard_map/muon/pallas_call | solution.py:452
  99.2 0.7 copy.3
Async XLA Ops:
  0.0 1.0 copy-start

commit v4 on v3

--- a/solution.py
+++ b/solution.py
@@ -21,6 +21,7 @@
 
 BLOCK = 288
 WIDTH = 256
+SHARE = BLOCK // 2
 PANEL = 4 * BLOCK
 HALF = PANEL // 2
 GROUP = 384
@@ -53,28 +54,29 @@
     ys_s, ys_r, yg_s, yg_r, zs_s, zs_r,
 ):
     row, col = lax.axis_index("row"), lax.axis_index("col")
-    y, x, z, k = row // 4, row % 4, col // 2, col % 2
+    y, x, z, k = lax.div(row, 4), lax.rem(row, 4), lax.div(col, 2), lax.rem(col, 2)
     first = k == 0
 
     def at_x(d):
-        return (y * 4 + (x + d) % 4, col)
+        return (y * 4 + lax.rem(x + d, 4), col)
 
     def at_y(d):
-        return (((y + d) % 4) * 4 + x, col)
+        return (lax.rem(y + d, 4) * 4 + x, col)
 
     def at_z(d):
-        return (row, ((z + d) % 16) * 2 + k)
+        return (row, lax.rem(z + d, 16) * 2 + k)
 
     other = (row, z * 2 + 1 - k)
+    ways, two_on = (at_z(1), at_z(15)), at_z(2)
 
     o_sum, o_all = jnp.where(first, x, y), jnp.where(first, y, x)
 
     def ring_sum(d):
-        t = (o_sum + d) % 4
+        t = lax.rem(o_sum + d, 4)
         return t, (jnp.where(first, y * 4 + t, t * 4 + x), col)
 
     def ring_all(d):
-        t = (o_all + d) % 4
+        t = lax.rem(o_all + d, 4)
         return (jnp.where(first, t * 4 + x, y * 4 + t), col)
 
     def send(src, dst, ss, rs, device):
@@ -91,8 +93,7 @@
         return c
 
     barrier = pltpu.get_barrier_semaphore()
-    peers = [at_x(d) for d in STEP4] + [at_y(d) for d in STEP4] + [other]
-    peers += [at_z(d) for d in (1, 15, 2, 14)]
+    peers = [at_x(1), at_x(3), at_y(1), at_y(3), at_z(1), at_z(15), other]
     for peer in peers:
         pl.semaphore_signal(barrier, inc=1, device_id=peer, device_id_type=MESH)
 
@@ -106,21 +107,54 @@
 
     pl.semaphore_wait(barrier, len(peers))
 
-    bulk = []
-    for i, d in enumerate(STEP4):
-        bulk.append(start(m_b, block(row_b, x), bulk_s.at[0, i], bulk_r.at[0, i], at_x(d)))
-        bulk.append(start(m_b, block(col_b, y), bulk_s.at[1, i], bulk_r.at[1, i], at_y(d)))
-
-    def pass_rows(src, t):
-        @pl.when(t // 2 != k)
+    def half_of(ref, t, h):
+        return ref.at[pl.ds(pl.multiple_of(t * BLOCK + h * SHARE, 16), SHARE), :]
+
+    rings = ((row_b, x, at_x(1), at_x(3)), (col_b, y, at_y(1), at_y(3)))
+
+    def bulk(j, way, step, onward=False):
+        panel, here, after, before = rings[j]
+        h = (way + step) % 2
+        t = here
+        if onward:
+            t = lax.rem(here + (3, 1)[way], 4)
+        src = half_of(panel, t, h) if onward else half_of(m_b, 0, h)
+        return send(
+            src, half_of(panel, t, h), bulk_s.at[j, way, step], bulk_r.at[j, way, step], (after, before)[way]
+        )
+
+    def came(j, way, step):
+        here = rings[j][1]
+        return lax.rem(here + ((3, 3, 2), (1, 1, 2))[way][step], 4), (way + step) % 2
+
+    for step in range(2):
+        for way in range(2):
+            for j in range(2):
+                sent.append(bulk(j, way, step))
+                sent[-1].start()
+
+    def pass_rows(src, t, h):
+        slot = lax.rem(t, 2) * 2 + h
+
+        @pl.when(lax.div(t, 2) != k)
         def _():
-            send(src, block(row_ob, t % 2), pass_s.at[0, t % 2], pass_r.at[0, t % 2], other).start()
-
-    def pass_cols(src, t):
-        send(src, block(col_ob, t), pass_s.at[1, t], pass_r.at[1, t], other).start()
-
-    pass_rows(m_b, x)
-    pass_cols(m_b, y)
+            send(src, half_of(row_ob, lax.rem(t, 2), h), pass_s.at[0, slot], pass_r.at[0, slot], other).start()
+
+    def pass_cols(src, t, h):
+        slot = t * 2 + h
+        send(src, half_of(col_ob, t, h), pass_s.at[1, slot], pass_r.at[1, slot], other).start()
+
+    def passed(j, slot):
+        ref = (row_ob, col_ob)[j]
+        at = ref.at[slot * SHARE : (slot + 1) * SHARE, :]
+        return send(at, at, pass_s.at[j, slot], pass_r.at[j, slot], other)
+
+    def pass_on(j, t, h):
+        (pass_rows, pass_cols)[j](half_of(rings[j][0], t, h), t, h)
+
+    for h in range(2):
+        pass_rows(half_of(m_b, 0, h), x, h)
+        pass_cols(half_of(m_b, 0, h), y, h)
 
     def exchange(stage, slots):
         for slot, device in slots:
@@ -137,18 +171,28 @@
     far = [(3, at_z(4)), (4, at_z(12))]
     along_x = [(6 + i, at_x(d)) for i, d in enumerate(STEP4)]
     along_y = [(9 + i, at_y(d)) for i, d in enumerate(STEP4)]
-    exchange(0, near)
+    exchange(0, near[:2])
 
     block(row_b, x)[...] = m_b[...]
     block(col_b, y)[...] = m_b[...]
     block(x_f, o_all)[...] = m_ref[...]
     part[STACK - 64 : STACK, :] = jnp.zeros((64, GROUP), F32)
 
-    for i, d in enumerate(STEP4):
-        bulk[2 * i].wait_recv()
-        pass_rows(block(row_b, (x + 4 - d) % 4), (x + 4 - d) % 4)
-        bulk[2 * i + 1].wait_recv()
-        pass_cols(block(col_b, (y + 4 - d) % 4), (y + 4 - d) % 4)
+    for way in range(2):
+        for j in range(2):
+            bulk(j, way, 0).wait_recv()
+            sent.append(bulk(j, way, 2, True))
+            sent[-1].start()
+            pass_on(j, *came(j, way, 0))
+    for step in (1, 2):
+        for way in range(2):
+            for j in range(2):
+                bulk(j, way, step).wait_recv()
+                pass_on(j, *came(j, way, step))
+
+    for slot, device in near[:2]:
+        send(tiles.at[0], tile_in.at[slot], tile_s.at[slot], tile_r.at[slot], device).wait_recv()
+    exchange(0, near[2:])
 
     wide = [
         start(m_ref, block(x_f, o_all), wide_s.at[i], wide_r.at[i], ring_all(d)) for i, d in enumerate(STEP4)
@@ -162,10 +206,10 @@
         return carry
 
     lax.fori_loop(0, GROUPS, gram_own, 0)
-    for t in range(2):
-        send(m_b, block(row_ob, t), pass_s.at[0, t], pass_r.at[0, t], other).wait_recv()
-    for t in range(4):
-        send(m_b, block(col_ob, t), pass_s.at[1, t], pass_r.at[1, t], other).wait_recv()
+    for slot in range(4):
+        passed(0, slot).wait_recv()
+    for slot in range(8):
+        passed(1, slot).wait_recv()
 
     def gram_other(n, carry):
         at = pl.ds(pl.multiple_of(n * GROUP, GROUP), GROUP)
@@ -175,7 +219,7 @@
     lax.fori_loop(0, GROUPS, gram_other, 0)
 
     def piece(c, p):
-        return pl.ds(pl.multiple_of((c + 32) % 16 * CHUNK + PARTS[p][0], 16), PARTS[p][1])
+        return pl.ds(pl.multiple_of(lax.rem(c + 32, 16) * CHUNK + PARTS[p][0], 16), PARTS[p][1])
 
     def inside(p):
         return pl.ds(PARTS[p][0], PARTS[p][1])
@@ -184,12 +228,12 @@
         ring = (ring_p, ring_m)[d]
         return send(
             ring.at[s, inside(p)], ring.at[s + 1, inside(p)],
-            rs_s.at[d, s, p], rs_r.at[d, s, p], (at_z(1), at_z(15))[d],
+            rs_s.at[d, s, p], rs_r.at[d, s, p], ways[d],
         )
 
     def jump(p):
         return send(
-            ring_p.at[0, inside(p)], ring_p.at[9, inside(p)], rs_s.at[0, 0, p], rs_r.at[0, 0, p], at_z(2)
+            ring_p.at[0, inside(p)], ring_p.at[9, inside(p)], rs_s.at[0, 0, p], rs_r.at[0, 0, p], two_on
         )
 
     for p in range(NP):
@@ -217,7 +261,6 @@
             minus_step(s, p)
         return carry
 
-    gathered(0, near)
     for p in range(NP):
         minus_step(1, p)
     for p in range(NP):
@@ -227,6 +270,8 @@
         ring_p[2, inside(p)] = total.astype(BF16)
         hop(0, 2, p).start()
         minus_step(2, p)
+    send(tiles.at[0], tile_in.at[2], tile_s.at[2], tile_r.at[2], two_on).wait_recv()
+    tiles[1] = tiles[0] + tile_in[0] + tile_in[1] + tile_in[2]
     lax.fori_loop(3, 4, reduce_step, 0)
     exchange(1, far)
     lax.fori_loop(4, 6, reduce_step, 0)
@@ -242,14 +287,14 @@
 
     def onward(d, s, p):
         at = gram.at[k, piece((z - s, z + s)[d], p)]
-        return send(at, at, ag_s.at[d, s, p], ag_r.at[d, s, p], (at_z(1), at_z(15))[d])
+        return send(at, at, ag_s.at[d, s, p], ag_r.at[d, s, p], ways[d])
 
     def arrived(d, s, p):
         at = gram.at[k, piece((z - s, z + s)[d], p)]
-        send(at, at, ag_s.at[d, s - 1, p], ag_r.at[d, s - 1, p], (at_z(1), at_z(15))[d]).wait_recv()
+        send(at, at, ag_s.at[d, s - 1, p], ag_r.at[d, s - 1, p], ways[d]).wait_recv()
 
     def chunk(c):
-        return pl.ds(pl.multiple_of((c + 32) % 16 * CHUNK, 16), CHUNK)
+        return pl.ds(pl.multiple_of(lax.rem(c + 32, 16) * CHUNK, 16), CHUNK)
 
     def swap(slot, c):
         at = gram.at[k, chunk(c)]
@@ -292,7 +337,7 @@
     for p in range(NP):
         arrived(0, 6, p)
         at = gram.at[k, piece(z - 6, p)]
-        send(at, at, ag_s.at[0, 7, p], ag_r.at[0, 7, p], at_z(2)).start()
+        send(at, at, ag_s.at[0, 7, p], ag_r.at[0, 7, p], two_on).start()
         onward(0, 6, p).start()
         arrived(1, 6, p)
         onward(1, 6, p).start()
@@ -427,10 +472,10 @@
 
     for c in sent:
         c.wait_send()
-    for t in range(2):
-        send(block(row_ob, t), block(row_ob, t), pass_s.at[0, t], pass_r.at[0, t], other).wait_send()
-    for t in range(4):
-        send(block(col_ob, t), block(col_ob, t), pass_s.at[1, t], pass_r.at[1, t], other).wait_send()
+    for slot in range(4):
+        passed(0, slot).wait_send()
+    for slot in range(8):
+        passed(1, slot).wait_send()
     for slot in range(16):
         swap(slot, z).wait_send()
     for copies in y_sum + y_gather:
@@ -476,8 +521,8 @@
             pltpu.VMEM((2, 3, BLOCK, SIDE), BF16),
             pltpu.VMEM((2, BLOCK, SIDE), F32),
             dma((13,)), dma((13,)),
-            dma((2, 3)), dma((2, 3)),
-            dma((2, 4)), dma((2, 4)),
+            dma((2, 2, 3)), dma((2, 2, 3)),
+            dma((2, 8)), dma((2, 8)),
             dma((3,)), dma((3,)),
             dma((2, 8, NP)), dma((2, 8, NP)),
             dma((2, 8, NP)), dma((2, 8, NP)),

time: 100 us -> 99.4 us (level)
  no operation moved by 1% of the time
where the time goes in v4:
time: 99.4 us; the launch traced here: 99.3 us
  Pallas kernels  97.6 us (98%)
  local copies, waits for them, and re-layouts  1.68 us (2%)
    pallas_call x1, Pallas kernels, body(): pl.pallas_call(kernel, out_shape=jax.ShapeDtypeStruct((BLOCK, WIDTH), F32...  97.6 us

profile of v4, /device:TPU:1, one launch (start us, length us, event | category | flops | bytes accessed | tf_op | source)
XLA Modules:
  0.0 99.3 jit_solution(2040600138747002068)
XLA Ops:
  0.0 0.0 copy-start
  0.0 1.0 copy-done
  1.0 97.6 %muon.1 = f32[288,256]{1,0:T(8,128)S(1)} custom-call(f32[288,256]{1,0:T(8,128)S(1)} %copy-done), custom_call_target="tpu_custom_call" | custom-call | tf_op jit(solution)/shard_map/muon/pallas_call | solution.py:497
  98.6 0.7 copy.3
Async XLA Ops:
  0.0 1.0 copy-start

commit v5 on v4

--- a/solution.py
+++ b/solution.py
@@ -67,7 +67,7 @@
         return (row, lax.rem(z + d, 16) * 2 + k)
 
     other = (row, z * 2 + 1 - k)
-    ways, two_on = (at_z(1), at_z(15)), at_z(2)
+    ways, two_on, two_back = (at_z(1), at_z(15)), at_z(2), at_z(14)
 
     o_sum, o_all = jnp.where(first, x, y), jnp.where(first, y, x)
 
@@ -231,19 +231,11 @@
             rs_s.at[d, s, p], rs_r.at[d, s, p], ways[d],
         )
 
-    def jump(p):
-        return send(
-            ring_p.at[0, inside(p)], ring_p.at[9, inside(p)], rs_s.at[0, 0, p], rs_r.at[0, 0, p], two_on
-        )
-
     for p in range(NP):
         ring_p[0, inside(p)] = part[piece(z + 8, p), :].astype(BF16)
-        jump(p).start()
+        hop(0, 0, p).start()
         ring_m[0, inside(p)] = part[piece(z - 7, p), :].astype(BF16)
         hop(1, 0, p).start()
-    for p in range(NP):
-        ring_p[1, inside(p)] = part[piece(z + 7, p), :].astype(BF16)
-        hop(0, 1, p).start()
 
     def plus_step(s, p):
         hop(0, s - 1, p).wait_recv()
@@ -261,15 +253,7 @@
             minus_step(s, p)
         return carry
 
-    for p in range(NP):
-        minus_step(1, p)
-    for p in range(NP):
-        jump(p).wait_recv()
-        hop(0, 1, p).wait_recv()
-        total = ring_p[2, inside(p)].astype(F32) + ring_p[9, inside(p)].astype(F32) + part[piece(z + 6, p), :]
-        ring_p[2, inside(p)] = total.astype(BF16)
-        hop(0, 2, p).start()
-        minus_step(2, p)
+    lax.fori_loop(1, 3, reduce_step, 0)
     send(tiles.at[0], tile_in.at[2], tile_s.at[2], tile_r.at[2], two_on).wait_recv()
     tiles[1] = tiles[0] + tile_in[0] + tile_in[1] + tile_in[2]
     lax.fori_loop(3, 4, reduce_step, 0)
@@ -326,21 +310,37 @@
     lax.fori_loop(1, 3, gather_step, 0)
     gathered(2, along_x)
     exchange(3, along_y)
-    lax.fori_loop(3, 5, gather_step, 0)
+    def leap(d, s, p):
+        at = gram.at[k, piece((z - s, z + s)[d], p)]
+        return send(at, at, ag_s.at[d, s + 1, p], ag_r.at[d, s + 1, p], (two_on, two_back)[d])
+
+    lax.fori_loop(3, 4, gather_step, 0)
+    for p in range(NP):
+        arrived(0, 4, p)
+        leap(0, 4, p).start()
+        onward(0, 4, p).start()
+        arrived(1, 4, p)
+        onward(1, 4, p).start()
+    swap(4, z - 4).start()
+    swap(12, z + 4).start()
     gathered(3, along_y)
     exchange(4, [(12, other)])
-    lax.fori_loop(5, 6, gather_step, 0)
+    for p in range(NP):
+        arrived(1, 5, p)
+        leap(1, 5, p).start()
+        onward(1, 5, p).start()
+        arrived(0, 5, p)
+    swap(5, z - 5).start()
+    swap(13, z + 5).start()
     gathered(4, [(12, other)])
     norm_squares = jnp.sum(tiles[5])
     factor = 0.6 * math.sqrt(ROWS) / (jnp.sqrt(jnp.full((8, 128), norm_squares, F32)) + 1e-07)
     factor = factor[0:1, 0:1]
     for p in range(NP):
         arrived(0, 6, p)
-        at = gram.at[k, piece(z - 6, p)]
-        send(at, at, ag_s.at[0, 7, p], ag_r.at[0, 7, p], two_on).start()
+        leap(0, 6, p).start()
         onward(0, 6, p).start()
         arrived(1, 6, p)
-        onward(1, 6, p).start()
     swap(6, z - 6).start()
     swap(14, z + 6).start()
 

time: 99.4 us -> 98.7 us (level)
  no operation moved by 1% of the time
where the time goes in v5:
time: 98.7 us; the launch traced here: 98.5 us
  Pallas kernels  96.9 us (98%)
  local copies, waits for them, and re-layouts  1.68 us (2%)
    pallas_call x1, Pallas kernels, body(): pl.pallas_call(kernel, out_shape=jax.ShapeDtypeStruct((BLOCK, WIDTH), F32...  96.9 us

profile of v5, /device:TPU:1, one launch (start us, length us, event | category | flops | bytes accessed | tf_op | source)
XLA Modules:
  0.0 98.5 jit_solution(16824318384282612573)
XLA Ops:
  0.0 0.0 copy-start
  0.0 1.0 copy-done
  1.0 96.9 %muon.1 = f32[288,256]{1,0:T(8,128)S(1)} custom-call(f32[288,256]{1,0:T(8,128)S(1)} %copy-done), custom_call_target="tpu_custom_call" | custom-call | tf_op jit(solution)/shard_map/muon/pallas_call | solution.py:497
  97.8 0.7 copy.3
Async XLA Ops:
  0.0 1.0 copy-start
